TPU v7x, 128 devices: a whole 4x4x4 slice. The times are simulated.
128 devices in a mesh: row: 8 (over z, core), col: 16 (over x, y).
Axes of the slice: x: 4, y: 4, z: 4, core: 2. Of those that a mesh axis runs over, the one named last changes fastest.
Arguments:
- features: bfloat16 [12, 8, 256, 256], P(None, 'row', 'col'), may hold values from -6 to 6
Outputs:
- schur: float32 [12, 8, 256, 6, 16, 256], P(None, 'row', None, None, 'col')
- panels: float32 [12, 8, 256, 512], P(None, 'row')
All inputs are finite; a program needn't handle non-finite values.
Results may differ from a plain program's by a relative error of at most 0.0033.
Values may be sent and summed in bfloat16 or wider, within the bound.
No kernel may reach another device: no remote copies, remote signals or barrier semaphores. Data moves between devices by JAX's collectives and lax.ppermute only.
A program may use at most 128 MiB of HBM per device.

v0:
```python
import jax
import jax.numpy as jnp
from jax import lax
from jax.sharding import PartitionSpec as P

kernel_gain = 2.0
epsilon = 1e-06


def spread(value, axis, source):
    kept = jnp.where(lax.axis_index(axis) == source, value, 0).astype(value.dtype)
    return lax.psum(kept, axis)


def per_device(features):
    row_count = lax.axis_size("row")
    col_count = lax.axis_size("col")
    own_row = lax.axis_index("row")
    own_col = lax.axis_index("col")
    floated = features.astype(jnp.float32)
    unit_rows = (
        floated * lax.rsqrt(jnp.sum(floated * floated, axis=-1, keepdims=True) + epsilon)
    ).astype(jnp.bfloat16)
    gathered = lax.all_gather(unit_rows, "col", axis=2, tiled=True)
    local_tiles = gathered.shape[0]
    tile_len = gathered.shape[2]
    feat_width = gathered.shape[3]
    stride = col_count // row_count
    grouped = gathered.reshape(local_tiles // stride, stride, tile_len, feat_width)
    chosen = lax.dynamic_index_in_dim(grouped, own_col // row_count, 1, keepdims=False)
    column_feats = spread(chosen, "row", own_col % row_count)
    across_tiles = column_feats.shape[0]
    row_points = gathered.reshape(local_tiles * tile_len, feat_width)
    col_points = column_feats.reshape(across_tiles * tile_len, feat_width)
    products = lax.dot_general(
        row_points, col_points, (((1,), (1,)), ((), ())), preferred_element_type=jnp.float32
    )
    row_global = jnp.arange(local_tiles, dtype=jnp.int32) * row_count + own_row
    col_global = jnp.arange(across_tiles, dtype=jnp.int32) * col_count + own_col
    coincide = (row_global[:, None] == col_global[None, :]).astype(jnp.float32)
    identity = jnp.eye(tile_len, dtype=jnp.float32)
    nugget = coincide[:, None, :, None] * identity[None, :, None, :]
    kernel = (
        jnp.exp(kernel_gain * (products - 1.0)).reshape(
            local_tiles, tile_len, across_tiles, tile_len
        )
        + nugget
    ).reshape(local_tiles * tile_len, across_tiles * tile_len)

    def outer(panel_rows, panel_cols, contract):
        return lax.dot_general(
            panel_rows,
            panel_cols,
            (((1,), (contract,)), ((), ())),
            precision=lax.Precision.HIGHEST,
            preferred_element_type=jnp.float32,
        )

    def factor_panel(panel_index, col_block):
        diag_start = panel_index // row_count * tile_len
        diagonal = col_block[diag_start : diag_start + tile_len]
        diag_all = spread(diagonal, "row", panel_index % row_count)
        factor = jnp.linalg.cholesky(diag_all)
        solved = lax.linalg.triangular_solve(
            factor, col_block, left_side=False, lower=True, transpose_a=True
        )
        pieces = solved.reshape(local_tiles, tile_len, tile_len)
        marker = row_global[:, None, None]
        pieces = jnp.where(
            marker == panel_index,
            factor[None],
            jnp.where(marker < panel_index, jnp.zeros_like(pieces), pieces),
        )
        panel_rows = spread(
            pieces.reshape(local_tiles * tile_len, tile_len), "col", panel_index % col_count
        )
        grouped_rows = panel_rows.reshape(local_tiles // stride, stride, tile_len, tile_len)
        picked = lax.dynamic_index_in_dim(grouped_rows, own_col // row_count, 1, keepdims=False)
        panel_cols = spread(picked, "row", own_col % row_count).reshape(
            across_tiles * tile_len, tile_len
        )
        contract = 1
        return (panel_rows, panel_cols, contract)

    def column_of(matrix, panel_index):
        start = panel_index // col_count * tile_len
        return matrix[:, start : start + tile_len]

    first = factor_panel(0, column_of(kernel, 0))
    after = kernel - outer(first[0], first[1], first[2])
    second = factor_panel(1, column_of(after, 1))
    schur = after - outer(second[0], second[1], second[2])
    both_rows = jnp.concatenate([first[0], second[0]], axis=1)
    return (
        schur.reshape(local_tiles, 1, tile_len, across_tiles, 1, tile_len),
        both_rows.reshape(local_tiles, 1, tile_len, 2 * tile_len),
    )


def solution(mesh):
    return jax.shard_map(
        per_device,
        mesh=mesh,
        in_specs=(P(None, "row", "col", None),),
        out_specs=(P(None, "row", None, None, "col", None), P(None, "row", None, None)),
        check_vma=False,
    )
```

profile of v0, /device:TPU:1, one launch (start us, length us, event | category | flops | bytes accessed | tf_op | source)
XLA Modules:
  0.0 863.3 jit_solution(536328949343994074)
XLA Ops:
  7.2 1.0 fusion.13
  8.2 1.6 fusion.14
  10.1 47.8 %all-gather.2.cloned.1.call-done = bf16[12,1,256,256]{3,2,0,1:T(8,128)(2,1)} async-done(((bf16[12,1,16,256]{3,2,0,1:T(8,128)(2,1)}), bf16[12,1,256,256]{3,2,0,1:T(8,128)(2,1)}) %all-gather.2.cloned.1.call-update) | async-done | bytes 1572880 | tf_op jit(solution)/shard_map/all_gather | solution.py:24
  57.9 2.1 dynamic-slice_select_fusion.2
  60.1 10.7 %broadcast_multiply_fusion = f32[12,256,6,256]{3,2,1,0:T(8,128)} fusion(f32[256,256]{1,0:T(8,128)S(1)} %fusion.12, f32[12,6]{1,0:T(8,128)S(1)} %compare_convert_fusion), kind=kLoop, calls=%fused_computation.7 | loop fusion | flops 4718592 | bytes 19136800 | tf_op jit(solution)/shard_map/mul | solution.py:42
  70.7 20.5 %copy.53 = f32[384,8,6,256]{3,1,2,0:T(8,128)} copy(f32[384,8,6,256]{3,2,1,0:T(8,128)} %bitcast.90) | data formatting | bytes 37748736
  91.3 18.8 %copy.29 = f32[3072,1536]{0,1:T(8,128)} copy(f32[3072,1536]{1,0:T(8,128)} %bitcast.91) | data formatting | bytes 37748736 | tf_op jit(solution)/shard_map/mul | solution.py:42
  110.1 11.3 %all-reduce.9.cloned.1.call-done = bf16[1536,256]{1,0:T(8,128)(2,1)} async-done(((bf16[1536,256]{1,0:T(8,128)(2,1)}), bf16[1536,256]{1,0:T(8,128)(2,1)}) %all-reduce.9.cloned.1.call-update) | async-done | bytes 786448 | tf_op jit(solution)/shard_map/psum | solution.py:12
  121.4 12.6 %exponential_add_fusion = f32[3072,1536]{0,1:T(8,128)} fusion(f32[3072,1536]{0,1:T(8,128)} %copy.29, bf16[3072,256]{1,0:T(8,128)(2,1)S(1)} %bitcast.99, bf16[1536,256]{1,0:T(8,128)(2,1)} %all-reduce.9.cloned.1.call-done), kind=kOutput, calls=%fused_computation.4 | convolution fusion | flops 2430074880 | bytes 40108032 | tf_op jit(solution)/shard_map/dot_general | solution.py:35
  134.0 1.7 slice_select_fusion.1
  136.1 58.9 %all-reduce.11.cloned.1.call-done = f32[256,256]{0,1:T(8,128)} async-done(((f32[256,256]{0,1:T(8,128)}), f32[256,256]{0,1:T(8,128)}) %all-reduce.11.cloned.1.call-update) | async-done | bytes 262160 | tf_op jit(solution)/shard_map/psum | solution.py:12
  195.0 1.1 copy.30
  196.1 1.0 fusion.9
  197.1 11.7 %cholesky.130 = f32[128,128]{1,0:T(8,128)S(1)} custom-call(f32[128,128]{1,0:T(8,128)S(1)} %cholesky.194), custom_call_target="Cholesky" | custom-call | tf_op jit(solution)/shard_map/jit(cholesky)/cholesky | solution.py:63
  208.9 9.8 %custom-call.13 = f32[1,128,128]{1,2,0:T(8,128)S(1)} custom-call(f32[1,128,128]{2,1,0:T(8,128)S(1)} %get-tuple-element.57), custom_call_target="InvertDiagBlocksLowerTriangular" | custom-call | tf_op jit(solution)/shard_map/jit(cholesky)/cholesky | solution.py:63
  219.2 11.7 %cholesky.147 = f32[128,128]{1,0:T(8,128)S(1)} custom-call(f32[128,128]{1,0:T(8,128)S(1)} %convolution_subtract_fusion.5), custom_call_target="Cholesky" | custom-call | tf_op jit(solution)/shard_map/jit(cholesky)/cholesky | solution.py:63
  232.9 4.0 while.4
  233.7 1.3 bitcast_dynamic-update-slice_fusion.4
  235.6 1.3 bitcast_dynamic-update-slice_fusion.4
  237.0 19.7 %custom-call.14 = f32[2,128,128]{1,2,0:T(8,128)S(1)} custom-call(f32[2,128,128]{2,1,0:T(8,128)S(1)} %get-tuple-element.18), custom_call_target="InvertDiagBlocksLowerTriangular" | custom-call | tf_op jit(solution)/shard_map/triangular_solve/custom-call.0 | solution.py:64
  256.6 2.9 fusion.6
  259.5 3.0 convolution_subtract_fusion.3
  262.5 1.5 fusion.19
  264.1 1.9 broadcast_in_dim.91
  266.0 3.5 copy.32
  269.5 4.1 fusion.1
  273.7 96.2 %all-reduce.13.cloned.1.call-done = f32[3072,256]{0,1:T(8,128)} async-done(((f32[3072,256]{0,1:T(8,128)}), f32[3072,256]{0,1:T(8,128)}) %all-reduce.13.cloned.1.call-update) | async-done | bytes 3145744 | tf_op jit(solution)/shard_map/psum | solution.py:12
  369.9 3.5 copy.49
  373.5 2.9 dynamic-slice_select_fusion.1
  376.4 61.9 %all-reduce.15.cloned.1.call-done = f32[1536,256]{1,0:T(8,128)} async-done(((f32[1536,256]{1,0:T(8,128)}), f32[1536,256]{1,0:T(8,128)}) %all-reduce.15.cloned.1.call-update) | async-done | bytes 1572880 | tf_op jit(solution)/shard_map/psum | solution.py:12
  438.4 18.7 %convolution_subtract_fusion.1 = f32[3072,1536]{0,1:T(8,128)S(1)} fusion(f32[3072,1536]{0,1:T(8,128)} %exponential_add_fusion, f32[3072,256]{0,1:T(8,128)S(1)} %copy-done.1, f32[1536,256]{1,0:T(8,128)} %all-reduce.15.cloned.1.call-done), kind=kOutput, calls=%fused_computation.6 | convolution fusion | flops 14500233216 | bytes 42467328 | tf_op jit(solution)/shard_map/dot_general | solution.py:51
  457.1 6.8 copy-done
  464.0 0.7 slice_select_fusion
  465.4 58.8 %all-reduce.17.cloned.1.call-done = f32[256,256]{0,1:T(8,128)} async-done(((f32[256,256]{0,1:T(8,128)}), f32[256,256]{0,1:T(8,128)}) %all-reduce.17.cloned.1.call-update) | async-done | bytes 262160 | tf_op jit(solution)/shard_map/psum | solution.py:12
  524.1 1.1 copy.35
  525.2 1.0 fusion.8
  526.2 0.7 copy-done.7
  526.9 11.7 %cholesky.164 = f32[128,128]{1,0:T(8,128)S(1)} custom-call(f32[128,128]{1,0:T(8,128)S(1)} %cholesky.197), custom_call_target="Cholesky" | custom-call | tf_op jit(solution)/shard_map/jit(cholesky)/cholesky | solution.py:63
  539.3 9.8 %custom-call.15 = f32[1,128,128]{1,2,0:T(8,128)S(1)} custom-call(f32[1,128,128]{2,1,0:T(8,128)S(1)} %get-tuple-element.53), custom_call_target="InvertDiagBlocksLowerTriangular" | custom-call | tf_op jit(solution)/shard_map/jit(cholesky)/cholesky | solution.py:63
  549.1 1.0 constant_dynamic-update-slice_fusion
  550.2 1.1 convolution_subtract_fusion.4
  551.3 11.7 %cholesky.181 = f32[128,128]{1,0:T(8,128)S(1)} custom-call(f32[128,128]{1,0:T(8,128)S(1)} %convolution_subtract_fusion.4), custom_call_target="Cholesky" | custom-call | tf_op jit(solution)/shard_map/jit(cholesky)/cholesky | solution.py:63
  563.1 0.7 compare_reduce_fusion
  564.9 0.8 fusion.10
  565.7 4.0 while.5
  566.5 1.3 bitcast_dynamic-update-slice_fusion.5
  568.4 1.3 bitcast_dynamic-update-slice_fusion.5
  569.7 0.6 copy-done.8
  570.3 20.5 %custom-call.16 = f32[2,128,128]{1,2,0:T(8,128)S(1)} custom-call(f32[2,128,128]{2,1,0:T(8,128)} %copy-done.8), custom_call_target="InvertDiagBlocksLowerTriangular" | custom-call | tf_op jit(solution)/shard_map/triangular_solve/custom-call.0 | solution.py:64
  590.8 2.9 fusion.4
  593.7 3.6 convolution_subtract_fusion.2
  597.3 2.7 fusion.15
  600.0 1.9 broadcast_in_dim.100
  601.9 3.5 copy.37
  605.5 5.2 fusion.3
  610.8 96.2 %all-reduce.19.cloned.1.call-done = f32[3072,256]{0,1:T(8,128)} async-done(((f32[3072,256]{0,1:T(8,128)}), f32[3072,256]{0,1:T(8,128)}) %all-reduce.19.cloned.1.call-update) | async-done | bytes 3145744 | tf_op jit(solution)/shard_map/psum | solution.py:12
  707.0 3.7 copy.50
  710.7 2.7 dynamic-slice_select_fusion
  713.5 5.1 pad_maximum_fusion
  718.6 6.7 copy.41
  725.4 50.1 %all-reduce.21.cloned.1.call-done = f32[1536,256]{1,0:T(8,128)} async-done(((f32[1536,256]{1,0:T(8,128)}), f32[1536,256]{1,0:T(8,128)}) %all-reduce.21.cloned.1.call-update) | async-done | bytes 1572880 | tf_op jit(solution)/shard_map/psum | solution.py:12
  775.5 21.6 %convolution_subtract_fusion = f32[3072,1536]{0,1:T(8,128)} fusion(f32[3072,1536]{0,1:T(8,128)} %copy-done, f32[3072,256]{0,1:T(8,128)S(1)} %copy-done.2, f32[1536,256]{1,0:T(8,128)} %all-reduce.21.cloned.1.call-done), kind=kOutput, calls=%fused_computation.5 | convolution fusion | flops 14500233216 | bytes 42467328 | tf_op jit(solution)/shard_map/dot_general | solution.py:51
  797.0 23.3 %reshape.189 = f32[12,1,256,6,1,256]{2,0,5,3,4,1:T(8,128)} reshape(f32[3072,1536]{0,1:T(8,128)} %convolution_subtract_fusion) | data formatting | bytes 37748736 | tf_op jit(solution)/shard_map/reshape | solution.py:95
  820.4 35.9 %copy.42 = f32[12,1,256,6,1,256]{5,4,3,2,1,0:T(1,128)} copy(f32[12,1,256,6,1,256]{2,0,5,3,4,1:T(8,128)} %reshape.189) | data formatting | bytes 37748736
  (71 shorter events, 6.0 us)
Async XLA Ops:
  7.2 50.8 %all-gather.2.cloned.1.call-start = ((), (), s32[]{:S(2)}) async-start(), calls=%async_computation | async-start | bytes 1671168 | tf_op jit(solution)/shard_map/all_gather | solution.py:24
  9.9 111.5 %all-reduce.9.cloned.1.call-start = ((), (), s32[]{:S(2)}) async-start(), calls=%async_computation.1 | async-start | bytes 1572864 | tf_op jit(solution)/shard_map/psum | solution.py:12
  60.0 135.0 %all-reduce.11.cloned.1.call-start = ((), (), s32[]{:S(2)}) async-start(), calls=%async_computation.2 | async-start | bytes 524288 | tf_op jit(solution)/shard_map/psum | solution.py:12
  91.3 30.1 %copy-start.4 = (bf16[12,1,256,256]{3,2,0,1:T(8,128)(2,1)S(1)}, bf16[12,1,256,256]{3,2,0,1:T(8,128)(2,1)}, u32[]{:S(2)}) copy-start(bf16[12,1,256,256]{3,2,0,1:T(8,128)(2,1)} %all-gather.2.cloned.1.call-done) | copy-start | bytes 4718596
  135.7 234.2 %all-reduce.13.cloned.1.call-start = ((), (), s32[]{:S(2)}) async-start(), calls=%async_computation.3 | async-start | bytes 6291456 | tf_op jit(solution)/shard_map/psum | solution.py:12
  273.6 164.7 %all-reduce.15.cloned.1.call-start = ((), (), s32[]{:S(2)}) async-start(), calls=%async_computation.4 | async-start | bytes 3145728 | tf_op jit(solution)/shard_map/psum | solution.py:12
  373.5 64.9 %copy-start.1 = (f32[3072,256]{0,1:T(8,128)S(1)}, f32[3072,256]{0,1:T(8,128)}, u32[]{:S(2)}) copy-start(f32[3072,256]{0,1:T(8,128)} %all-reduce.13.cloned.1.call-done) | copy-start | bytes 9437188
  376.4 147.7 %all-reduce.17.cloned.1.call-start = ((), (), s32[]{:S(2)}) async-start(), calls=%async_computation.5 | async-start | bytes 524288 | tf_op jit(solution)/shard_map/psum | solution.py:12
  457.1 6.9 copy-start
  464.7 242.3 %all-reduce.19.cloned.1.call-start = ((), (), s32[]{:S(2)}) async-start(), calls=%async_computation.6 | async-start | bytes 6291456 | tf_op jit(solution)/shard_map/psum | solution.py:12
  526.2 0.7 copy-start.7
  563.1 1.9 copy-start.5
  569.7 0.7 copy-start.8
  593.7 6.3 copy-start.3
  593.7 6.3 copy-start.6
  610.7 164.7 %all-reduce.21.cloned.1.call-start = ((), (), s32[]{:S(2)}) async-start(), calls=%async_computation.7 | async-start | bytes 3145728 | tf_op jit(solution)/shard_map/psum | solution.py:12
  718.6 56.8 %copy-start.2 = (f32[3072,256]{0,1:T(8,128)S(1)}, f32[3072,256]{0,1:T(8,128)}, u32[]{:S(2)}) copy-start(f32[3072,256]{0,1:T(8,128)} %all-reduce.19.cloned.1.call-done) | copy-start | bytes 9437188
Sparse Core Ops, SparseCore 0:
  10.7 47.1 all-gather.1
  60.8 60.4 all-reduce.8
  135.8 59.1 all-reduce.10
  273.8 96.1 all-reduce.12
  376.5 61.8 all-reduce.14
  464.8 59.2 all-reduce.16
  610.9 96.1 all-reduce.18
  713.6 61.8 all-reduce.20
where the time goes:
time: 872 us; the launch traced here: 863 us
  waiting for transfers between devices  481 us (55%)
  other arithmetic  149 us (17%)
  local copies, waits for them, and re-layouts  142 us (16%)
  matrix products  72.1 us (8%)
  between operations  17.1 us (2%)
    psum x7, waiting for transfers between devices, spread(): return lax.psum(kept, axis)  433 us
    another operation x13, other arithmetic, factor_panel(): factor = jnp.linalg.cholesky(diag_all)  68.5 us
    unnamed x20, local copies, waits for them, and re-layouts  64.6 us
    all_gather x1, waiting for transfers between devices, per_device(): gathered = lax.all_gather(unit_rows, 'col', axis=2, tiled=True)  47.8 us
    another operation x5, other arithmetic, factor_panel(): lax.linalg.triangular_solve(factor, col_block, left_side=False, lower=Tru...  40.9 us
    dot_general x2, matrix products, outer(): lax.dot_general(panel_rows, panel_cols, (((1,), (contract,)), ((), ())),...  40.3 us
    reshape x1, local copies, waits for them, and re-layouts, per_device(): schur.reshape(local_tiles, 1, tile_len, across_tiles, 1, tile_len)  23.3 us
    select_n x7, other arithmetic, spread(): jnp.where(lax.axis_index(axis) == source, value, 0).astype(value.dtype)  19.4 us
  transfers between devices with their start and end apart: 8, of which 8 were waited for; matrix products, arithmetic and copies ran while one was open for 7% of the time, Pallas kernels for 0%

commit v1 on v0

v1 whole, which is shorter than its diff:
```python
import functools

import jax
import jax.numpy as jnp
from jax import lax
from jax.experimental import pallas as pl
from jax.experimental.pallas import tpu as pltpu
from jax.sharding import PartitionSpec as P

T = 256
N = 2 * T
B = 128
G = 8
BF = jnp.bfloat16
F32 = jnp.float32
SCALE = 2.0 * 1.4426950408889634
epsilon = 1e-06


def dot_nt(a, b):
    return lax.dot_general(a, b, (((1,), (1,)), ((), ())), preferred_element_type=F32)


def split(x):
    hi = x.astype(BF)
    return hi, (x - hi.astype(F32)).astype(BF)


def kern(u, v):
    return jnp.exp2(SCALE * dot_nt(u, v) - SCALE)


def normal(raw):
    f = raw.astype(F32)
    return (f * lax.rsqrt(jnp.sum(f * f, axis=-1, keepdims=True) + epsilon)).astype(BF)


def dot3(a, b, dims):
    ah, al = split(a)
    bh, bl = split(b)
    d = lambda x, y: lax.dot_general(x, y, (dims, ((), ())), preferred_element_type=F32)
    return d(ah, bh) + d(al, bh) + d(ah, bl)


def factor_block(a):
    eye = (lax.broadcasted_iota(jnp.int32, (B, B), 0) == lax.broadcasted_iota(jnp.int32, (B, B), 1)).astype(F32)
    n_g = B // G
    groups_a = [a[G * g : G * g + G] for g in range(n_g)]
    groups_b = [eye[G * g : G * g + G] for g in range(n_g)]
    out = []
    for g in range(n_g):
        cols = [
            [jnp.broadcast_to(groups_a[i][:, G * g + k : G * g + k + 1], (G, B)) for i in range(g, n_g)]
            for k in range(G)
        ]
        rows_a = [groups_a[g][k : k + 1] for k in range(G)]
        rows_b = [groups_b[g][k : k + 1] for k in range(G)]
        facs = []
        for k in range(G):
            scale = lax.rsqrt(cols[k][0][k : k + 1])
            fac = [x * scale for x in cols[k]]
            facs.append(fac)
            rows_a[k] = rows_a[k] * scale
            rows_b[k] = rows_b[k] * scale
            for m in range(k + 1, G):
                piv = fac[0][m : m + 1]
                cols[m] = [x - f * piv for x, f in zip(cols[m], fac)]
                rows_a[m] = rows_a[m] - piv * rows_a[k]
                rows_b[m] = rows_b[m] - piv * rows_b[k]
        out.append(jnp.concatenate(rows_b, axis=0))
        for i in range(g + 1, n_g):
            ga, gb = groups_a[i], groups_b[i]
            for k in range(G):
                ga = ga - facs[k][i - g] * rows_a[k]
                gb = gb - facs[k][i - g] * rows_b[k]
            groups_a[i], groups_b[i] = ga, gb
    return jnp.concatenate(out, axis=0)


def thrice(x, left):
    hi, lo = split(x)
    return jnp.concatenate([hi, lo, hi] if left else [hi, hi, lo], axis=1)


def picked(flag, second, mine, other):
    return jnp.where(flag, mine, other) if second else jnp.where(flag, other, mine)


def eliminate(top, k):
    w = dot3(top, k[:B, B:], ((1,), (0,)))
    return w, k[B:, B:] - dot3(w, w, ((0,), (0,)))


def joined(top, w, bottom):
    corner = dot3(bottom, dot3(w, top, ((0,), (0,))), ((1,), (0,)))
    return jnp.concatenate(
        [jnp.concatenate([top, jnp.zeros((B, B), F32)], axis=1), jnp.concatenate([-corner, bottom], axis=1)], axis=0
    )


def identity():
    return (lax.broadcasted_iota(jnp.int32, (T, T), 0) == lax.broadcasted_iota(jnp.int32, (T, T), 1)).astype(F32)


def factor_start(pos, mine, other, u0, top, w, rest):
    x = pos[1] // 4
    inner = jnp.logical_or(x == 1, x == 2)
    for t in range(2):
        for c in range(16):
            x, y = c // 4, c % 4
            block = picked(inner, int(x in (1, 2)), mine[x // 2, y, t], other[x // 2, y, t])
            u0[t * T + c * 16 : t * T + c * 16 + 16, :] = normal(block)
    u = u0[:T, :]
    k = kern(u, u) + identity()
    top[...] = factor_block(k[:B, :B])
    w[...], rest[...] = eliminate(top[...], k)


def factor_middle(u0, top, w, rest, x0, lx, d1):
    u = u0[...]
    k10 = kern(u[T:], u[:T])
    k11 = kern(u[T:], u[T:]) + identity()
    x = joined(top[...], w[...], factor_block(rest[...]))
    x0[...] = thrice(x, False)
    low = dot_nt(thrice(k10, True), x0[...])
    lx[...] = dot3(low, x, ((1,), (0,)))
    d1[...] = k11 - dot_nt(thrice(low, True), thrice(low, False))


def factor_next(d1, top, w, rest):
    d = d1[...]
    top[...] = factor_block(d[:B, :B])
    w[...], rest[...] = eliminate(top[...], d)


def factor_end(top, w, rest, lx, x1):
    x = joined(top[...], w[...], factor_block(rest[...]))
    x1[...] = thrice(jnp.concatenate([-dot3(x, lx[...], ((1,), (0,))), x], axis=1), False)


def factor_call(kernel, name, outs, *args):
    vmem = pl.BlockSpec(memory_space=pltpu.VMEM)
    place = lambda a: pl.BlockSpec(memory_space=pltpu.SMEM) if a.dtype == jnp.int32 else vmem
    return pl.pallas_call(
        kernel,
        out_shape=[jax.ShapeDtypeStruct(*o) for o in outs],
        in_specs=[place(a) for a in args],
        out_specs=[vmem] * len(outs),
        compiler_params=pltpu.CompilerParams(vmem_limit_bytes=16 * 2**20),
        cost_estimate=pl.CostEstimate(flops=4 * 10**9, bytes_accessed=10**6, transcendentals=T * N),
        name=name,
    )(*args)


def panel_rows(k, xs):
    kh, kl = split(k)
    out = []
    for b in range(2):
        n = (b + 1) * T
        out.append(dot_nt(jnp.concatenate([kh[:, :n], kl[:, :n], kh[:, :n]], axis=1), xs[b][...]))
    return out


def schur_kernel(pos, row_mine, row_other, col_mine, col_other, u0, x0, x1, schur, pan, pc, uc, *, tiles):
    step = pl.program_id(0)
    r, c = pos[0], pos[1]
    height = tiles * T

    @pl.when(step == 0)
    def _():
        core = r % 2 == 1
        for j in range(6):
            for s in range(16):
                z, e = s // 4, s % 2
                low, high = col_mine[z, e, j], col_other[z, e, j]
                block = picked(core, (s // 2) % 2, low, high)
                uc[j, s * 16 : s * 16 + 16, :] = normal(block)
            k = kern(uc[j], u0[...])
            if j == 0:
                rows = lax.broadcasted_iota(jnp.int32, (T, N), 0) + c * T
                k = k + (rows == lax.broadcasted_iota(jnp.int32, (T, N), 1)).astype(F32)
            (h0, l0), (h1, l1) = [split(p) for p in panel_rows(k, (x0, x1))]
            pc[j] = jnp.concatenate([h0, h1, h0, h1, l0, l1], axis=1)

    x_hi = c // 4 >= 2
    blocks = []
    for t in range(tiles):
        for s in range(16):
            x, y = s // 4, s % 4
            low, high = row_mine[x % 2, y, t], row_other[x % 2, y, t]
            blocks.append(picked(x_hi, x // 2, low, high))
    u = normal(jnp.concatenate(blocks, axis=0))
    k = kern(u, u0[...])
    rows = lax.broadcasted_iota(jnp.int32, (height, N), 0)
    cols = lax.broadcasted_iota(jnp.int32, (height, N), 1)
    shift = jnp.where(jnp.logical_and(step == 0, r < 2), r * T, N)
    rows = rows + jnp.where(rows < T, shift, N)
    k = k + (rows == cols).astype(F32)
    p = jnp.concatenate(panel_rows(k, (x0, x1)), axis=1)
    p = jnp.where(rows >= cols, p, 0.0)
    for t in range(tiles):
        pan[t] = p[t * T : (t + 1) * T]
    hi, lo = split(p)
    left = jnp.concatenate([hi, lo, hi], axis=1)
    for j in range(6):
        s = kern(u, uc[j]) - dot_nt(left, pc[j])
        for t in range(tiles):
            for h in range(2):
                schur[pl.ds(t * T * 12 + j * 2 + h, T, stride=12), :] = s[t * T : (t + 1) * T, h * 128 : h * 128 + 128]
    for t in range(tiles):
        a = step * tiles + t

        @pl.when(jnp.logical_and(r == c % 8, (a - c // 8) % 2 == 0))
        def _():
            j = (a - c // 8) // 2
            for h in range(2):
                where = pl.ds(t * T * 12 + j * 2 + h, T, stride=12)
                i = lax.broadcasted_iota(jnp.int32, (T, 128), 0)
                l = lax.broadcasted_iota(jnp.int32, (T, 128), 1) + h * 128
                schur[where, :] = schur[where, :] + (i == l).astype(F32)


def schur_call(pos, row_mine, row_other, col_mine, col_other, u0, x0, x1, tiles=2):
    full = lambda a: pl.BlockSpec(a.shape, lambda i, _: (0,) * a.ndim)
    rows = pl.BlockSpec((2, 4, tiles, 16, T), lambda i, _: (0, 0, i, 0, 0))
    return pl.pallas_call(
        functools.partial(schur_kernel, tiles=tiles),
        grid_spec=pltpu.PrefetchScalarGridSpec(
            num_scalar_prefetch=1,
            grid=(12 // tiles,),
            in_specs=[rows, rows] + [full(a) for a in (col_mine, col_other, u0, x0, x1)],
            out_specs=[
                pl.BlockSpec((tiles * T * 12, 128), lambda i, _: (i, 0)),
                pl.BlockSpec((tiles, T, N), lambda i, _: (i, 0, 0)),
            ],
            scratch_shapes=[pltpu.VMEM((6, T, 6 * T), BF), pltpu.VMEM((6, T, T), BF)],
        ),
        out_shape=[
            jax.ShapeDtypeStruct((12 * T * 12, 128), F32),
            jax.ShapeDtypeStruct((12, T, N), F32),
        ],
        compiler_params=pltpu.CompilerParams(vmem_limit_bytes=40 * 2**20, dimension_semantics=("arbitrary",)),
        cost_estimate=pl.CostEstimate(flops=24 * 10**9, bytes_accessed=30 * 10**6, transcendentals=7 * 10**6),
        name="schur",
    )(pos, row_mine, row_other, col_mine, col_other, u0, x0, x1)


def swap_row(value, flip_z, flip_core):
    pairs = [(r, (((r >> 1) ^ flip_z) << 1) | ((r & 1) ^ flip_core)) for r in range(8)]
    return lax.ppermute(value, "row", pairs)


def swap_col(value, flip_x, flip_y):
    pairs = [(c, (((c >> 2) ^ flip_x) << 2) | ((c & 3) ^ flip_y)) for c in range(16)]
    return lax.ppermute(value, "col", pairs)


def ordered(mine, other, second):
    return jnp.stack([jnp.where(second, other, mine), jnp.where(second, mine, other)])


def after(value, *earlier):
    return lax.optimization_barrier((value,) + earlier)[0]


def per_device(features):
    r = lax.axis_index("row")
    c = lax.axis_index("col")
    z, core = r // 2, r % 2
    x, y = c // 4, c % 4
    pos = jnp.stack([r, c]).astype(jnp.int32)
    own = features[:, 0]

    together = lambda *values: lax.optimization_barrier(values)

    first_a = own[0]
    first_b = swap_row(first_a, 0, 1)
    rows_b = swap_col(own, 0, 1)
    first = ordered(first_a, first_b, core == 1)

    got = swap_row(first, 1, 0)
    first, rows_b = together(jnp.where(z % 2 == 1, got, first), rows_b)

    got = swap_row(first, 3, 0)
    rows = ordered(own, rows_b, y % 2 == 1)
    pair = rows.reshape(2, 6, 2, 16, T)
    rows_b = swap_col(rows, 0, 3)
    first, rows_b = together(jnp.where(z >= 2, got, first), rows_b)

    first_b = swap_col(first, 0, 1)
    rows = ordered(rows, rows_b, y >= 2).reshape(4, 12, 16, T)
    rows_b = swap_col(rows, 1, 0)
    first = ordered(first, first_b, y % 2 == 1)

    first_b = swap_col(first, 0, 3)
    first = ordered(first, first_b, y >= 2).reshape(4, 2, 16, T)

    first_b = swap_col(first, 3, 0)
    first, rows_b = together(ordered(first, first_b, x >= 2), rows_b)

    first_b = swap_col(first, 1, 0)
    rows = ordered(rows, rows_b, x % 2 == 1)
    rows_b = swap_col(rows, 3, 0)
    pair = after(jnp.where(c % 2 == 1, pair[:, :, 1], pair[:, :, 0]), first)
    route = [(q * 16 + s, (s // 2) * 16 + (s % 2) * 8 + q) for q in range(8) for s in range(16)]
    cols = lax.ppermute(pair, ("row", "col"), route)

    small = [((B, B), F32)] * 3
    u0, *state = factor_call(factor_start, "factor_start", [((N, T), BF)] + small, pos, first, first_b)
    u0, cols = together(u0, cols)
    cols_b = swap_row(cols, 1, 0)
    x0, lx, d1 = factor_call(
        factor_middle, "factor_middle", [((T, 3 * T), BF), ((T, T), F32), ((T, T), F32)], u0, *state
    )
    d1, cols_b = together(d1, cols_b)
    cols = ordered(cols, cols_b, z % 2 == 1)
    cols_b = swap_row(cols, 3, 0)
    state = factor_call(factor_next, "factor_next", small, d1)
    *state, cols_b = together(*state, cols_b)
    cols = ordered(cols, cols_b, z >= 2).reshape(4, 2, 6, 16, T)
    cols_b = swap_row(cols, 0, 1)
    (x1,) = factor_call(factor_end, "factor_end", [((T, 6 * T), BF)], *state, lx)

    schur, panels = schur_call(pos, rows, rows_b, cols, cols_b, u0, x0, x1)
    return schur.reshape(12, 1, T, 6, 1, T), panels[:, None]


def solution(mesh):
    return jax.shard_map(
        per_device,
        mesh=mesh,
        in_specs=(P(None, "row", "col", None),),
        out_specs=(P(None, "row", None, None, "col", None), P(None, "row", None, None)),
        check_vma=False,
    )
```

time: 872 us -> 97.4 us (0.11)
  waiting for transfers between devices: 481 us -> 12.9 us
  other arithmetic: 149 us -> 2.23 us
  local copies, waits for them, and re-layouts: 142 us -> 0.7 us
  matrix products: 72.1 us -> 0 us
  Pallas kernels: 0 us -> 48.8 us
  starting transfers between devices: 0.91 us -> 31.7 us
  between operations: 17.1 us -> 0.8 us
    psum x7 -> x0, waiting for transfers between devices: 433 us -> none  [spread(): return lax.psum(kept, axis)]
    another operation x18, other arithmetic: 109 us -> 1.28 us  [the longest x17 1.21 us: ordered(): jnp.stack([jnp.where(second, other, mine), jnp.where(second, mine, other)])]
    unnamed x20 -> x0, local copies, waits for them, and re-layouts: 64.6 us -> none
    dot_general x3 -> x0, matrix products: 52.9 us -> none  [the longest x2 40.3 us: outer(): lax.dot_general(panel_rows, panel_cols, (((1,), (contract,)), ((), ())),...]
    pallas_call x0 -> x5, Pallas kernels: none -> 48.8 us  [the longest x1 30 us: schur_call(): pl.pallas_call(functools.partial(schur_kernel, tiles=tiles), grid_spec=pl...]
    all_gather x1 -> x0, waiting for transfers between devices: 47.8 us -> none  [per_device(): gathered = lax.all_gather(unit_rows, 'col', axis=2, tiled=True)]
    ppermute x0 -> x15, starting transfers between devices: none -> 31.7 us  [the longest x8 13.6 us: swap_col(): return lax.ppermute(value, 'col', pairs)]
    reshape x3 -> x0, local copies, waits for them, and re-layouts: 30.6 us -> none  [the longest x1 23.3 us: per_device(): schur.reshape(local_tiles, 1, tile_len, across_tiles, 1, tile_len)]
  transfers between devices with their start and end apart: 8 -> 15, of which waited for: 8 -> 7; matrix products, arithmetic and copies ran while one was open for 7% -> 2% of each run, Pallas kernels for 0% -> 19%
where the time goes in v1:
time: 97.4 us; the launch traced here: 97.2 us
  Pallas kernels  48.8 us (50%)
  starting transfers between devices  31.7 us (33%)
  waiting for transfers between devices  12.9 us (13%)
  other arithmetic  2.23 us (2%)
    pallas_call x1, Pallas kernels, schur_call(): pl.pallas_call(functools.partial(schur_kernel, tiles=tiles), grid_spec=pl...  30 us
    pallas_call x4, Pallas kernels, factor_call(): pl.pallas_call(kernel, out_shape=[jax.ShapeDtypeStruct(*o) for o in outs]...  18.8 us
    ppermute x8, starting transfers between devices, swap_col(): return lax.ppermute(value, 'col', pairs)  13.6 us
    ppermute x6, starting transfers between devices, swap_row(): return lax.ppermute(value, 'row', pairs)  10.6 us
    ppermute x8, waiting for transfers between devices, swap_col(): return lax.ppermute(value, 'col', pairs)  9.14 us
    ppermute x1, starting transfers between devices, per_device(): cols = lax.ppermute(pair, ('row', 'col'), route)  7.55 us
    ppermute x6, waiting for transfers between devices, swap_row(): return lax.ppermute(value, 'row', pairs)  3.77 us
  transfers between devices with their start and end apart: 15, of which 7 were waited for; matrix products, arithmetic and copies ran while one was open for 2% of the time, Pallas kernels for 19%

profile of v1, /device:TPU:1, one launch (start us, length us, event | category | flops | bytes accessed | tf_op | source)
XLA Modules:
  0.0 97.2 jit_solution(7879705008147950499)
XLA Ops:
  0.6 0.7 slice_bitcast_fusion
  1.3 1.4 %collective-permute-start = (bf16[16,256]{1,0:T(8,128)(2,1)S(1)}, bf16[16,256]{1,0:T(8,128)(2,1)S(1)}, u32[]{:S(2)}, u32[]{:S(2)}) collective-permute-start(bf16[16,256]{1,0:T(8,128)(2,1)S(1)} %slice_bitcast_fusion), channel_id=1, source_target_pairs={{0,16},{16,0},{32,48},{48,32},{64,80},{80,64},{96,112},{112,96},{1... | collective-permute-start | bytes 24584 | tf_op jit(solution)/shard_map/ppermute | solution.py:250
  2.8 1.4 %collective-permute-start.2 = (bf16[12,16,256]{2,1,0:T(8,128)(2,1)}, bf16[12,16,256]{2,1,0:T(8,128)(2,1)S(1)}, u32[]{:S(2)}, u32[]{:S(2)}) collective-permute-start(bf16[12,16,256]{2,1,0:T(8,128)(2,1)} %bitcast.80), channel_id=1, source_target_pairs={{0,1},{1,0},{2,3},{3,2},{4,5},{5,4},{6,7},{7,6},{8,9},{9,8},{10,11... | collective-permute-start | bytes 294920 | tf_op jit(solution)/shard_map/ppermute | solution.py:255
  4.1 0.0 collective-permute-done
  4.1 0.7 select_bitcast_fusion.15
  4.9 1.6 %collective-permute-start.1 = (bf16[2,16,256]{2,1,0:T(8,128)(2,1)S(1)}, bf16[2,16,256]{2,1,0:T(8,128)(2,1)S(1)}, u32[]{:S(2)}, u32[]{:S(2)}) collective-permute-start(bf16[2,16,256]{2,1,0:T(8,128)(2,1)S(1)} %pad_maximum_fusion.9), channel_id=1, source_target_pairs={{0,32},{16,48},{32,0},{48,16},{64,96},{80,112},{96,64},{112,80},{1... | collective-permute-start | bytes 49160 | tf_op jit(solution)/shard_map/ppermute | solution.py:250
  6.5 0.1 pad_add_fusion.pos
  6.6 1.2 %collective-permute-done.1 = bf16[2,16,256]{2,1,0:T(8,128)(2,1)S(1)} collective-permute-done((bf16[2,16,256]{2,1,0:T(8,128)(2,1)S(1)}, bf16[2,16,256]{2,1,0:T(8,128)(2,1)S(1)}, u32[]{:S(2)}, u32[]{:S(2)}) %collective-permute-start.1) | collective-permute-done | bytes 16416 | tf_op jit(solution)/shard_map/ppermute | solution.py:250
  7.8 0.0 collective-permute-done.2
  7.8 3.8 %collective-permute-start.3 = (bf16[2,16,256]{2,1,0:T(8,128)(2,1)S(1)}, bf16[2,16,256]{2,1,0:T(8,128)(2,1)S(1)}, u32[]{:S(2)}, u32[]{:S(2)}) collective-permute-start(bf16[2,16,256]{2,1,0:T(8,128)(2,1)S(1)} %broadcast_select_fusion.2), channel_id=1, source_target_pairs={{0,96},{16,112},{32,64},{48,80},{64,32},{80,48},{96,0},{112,16},{1... | collective-permute-start | bytes 49160 | tf_op jit(solution)/shard_map/ppermute | solution.py:250
  11.6 0.9 broadcast_select_fusion.1
  12.6 2.4 %collective-permute-start.4 = (bf16[2,12,16,256]{3,2,1,0:T(8,128)(2,1)S(1)}, bf16[2,12,16,256]{3,2,1,0:T(8,128)(2,1)S(1)}, u32[]{:S(2)}, u32[]{:S(2)}) collective-permute-start(bf16[2,12,16,256]{3,2,1,0:T(8,128)(2,1)S(1)} %pad_maximum_fusion.3), channel_id=1, source_target_pairs={{0,3},{1,2},{2,1},{3,0},{4,7},{5,6},{6,5},{7,4},{8,11},{9,10},{10,... | collective-permute-start | bytes 589832 | tf_op jit(solution)/shard_map/ppermute | solution.py:255
  15.0 0.0 collective-permute-done.3
  15.0 3.8 %collective-permute-done.4 = bf16[2,12,16,256]{3,2,1,0:T(8,128)(2,1)S(1)} collective-permute-done((bf16[2,12,16,256]{3,2,1,0:T(8,128)(2,1)S(1)}, bf16[2,12,16,256]{3,2,1,0:T(8,128)(2,1)S(1)}, u32[]{:S(2)}, u32[]{:S(2)}) %collective-permute-start.4) | collective-permute-done | bytes 196640 | tf_op jit(solution)/shard_map/ppermute | solution.py:255
  18.8 0.0 collective-permute-start.5
  18.9 2.6 %collective-permute-done.5 = bf16[2,16,256]{2,1,0:T(8,128)(2,1)S(1)} collective-permute-done((bf16[2,16,256]{2,1,0:T(8,128)(2,1)S(1)}, bf16[2,16,256]{2,1,0:T(8,128)(2,1)S(1)}, u32[]{:S(2)}, u32[]{:S(2)}) %collective-permute-start.5) | collective-permute-done | bytes 16416 | tf_op jit(solution)/shard_map/ppermute | solution.py:255
  21.4 2.5 %collective-permute-start.6 = (bf16[2,2,16,256]{3,2,1,0:T(8,128)(2,1)S(1)}, bf16[2,2,16,256]{3,2,1,0:T(8,128)(2,1)S(1)}, u32[]{:S(2)}, u32[]{:S(2)}) collective-permute-start(bf16[2,2,16,256]{3,2,1,0:T(8,128)(2,1)S(1)} %pad_maximum_fusion.8), channel_id=1, source_target_pairs={{0,3},{1,2},{2,1},{3,0},{4,7},{5,6},{6,5},{7,4},{8,11},{9,10},{10,... | collective-permute-start | bytes 98312 | tf_op jit(solution)/shard_map/ppermute | solution.py:255
  24.0 1.3 %collective-permute-start.8 = (bf16[4,12,16,256]{3,2,1,0:T(8,128)(2,1)S(1)}, bf16[4,12,16,256]{3,2,1,0:T(8,128)(2,1)S(1)}, u32[]{:S(2)}, u32[]{:S(2)}) collective-permute-start(bf16[4,12,16,256]{3,2,1,0:T(8,128)(2,1)S(1)} %bitcast.72), channel_id=1, source_target_pairs={{0,4},{1,5},{2,6},{3,7},{4,0},{5,1},{6,2},{7,3},{8,12},{9,13},{10,... | collective-permute-start | bytes 1179656 | tf_op jit(solution)/shard_map/ppermute | solution.py:255
  25.3 0.2 collective-permute-done.6
  25.5 2.6 %collective-permute-start.7 = (bf16[4,2,16,256]{3,2,1,0:T(8,128)(2,1)S(1)}, bf16[4,2,16,256]{3,2,1,0:T(8,128)(2,1)S(1)}, u32[]{:S(2)}, u32[]{:S(2)}) collective-permute-start(bf16[4,2,16,256]{3,2,1,0:T(8,128)(2,1)S(1)} %bitcast.79), channel_id=1, source_target_pairs={{0,12},{1,13},{2,14},{3,15},{4,8},{5,9},{6,10},{7,11},{8,4},{9,5},... | collective-permute-start | bytes 196616 | tf_op jit(solution)/shard_map/ppermute | solution.py:255
  28.1 1.8 %collective-permute-done.7 = bf16[4,2,16,256]{3,2,1,0:T(8,128)(2,1)S(1)} collective-permute-done((bf16[4,2,16,256]{3,2,1,0:T(8,128)(2,1)S(1)}, bf16[4,2,16,256]{3,2,1,0:T(8,128)(2,1)S(1)}, u32[]{:S(2)}, u32[]{:S(2)}) %collective-permute-start.7) | collective-permute-done | bytes 65568 | tf_op jit(solution)/shard_map/ppermute | solution.py:255
  30.0 0.7 collective-permute-done.8
  30.7 1.2 %collective-permute-start.10 = (bf16[2,4,2,16,256]{4,3,2,1,0:T(8,128)(2,1)S(1)}, bf16[2,4,2,16,256]{4,3,2,1,0:T(8,128)(2,1)S(1)}, u32[]{:S(2)}, u32[]{:S(2)}) collective-permute-start(bf16[2,4,2,16,256]{4,3,2,1,0:T(8,128)(2,1)S(1)} %pad_maximum_fusion.5.mine), channel_id=1, source_target_pairs={{0,4},{1,5},{2,6},{3,7},{4,0},{5,1},{6,2},{7,3},{8,12},{9,13},{10,... | collective-permute-start | bytes 393224 | tf_op jit(solution)/shard_map/ppermute | solution.py:255
  31.9 7.5 %collective-permute-start.11 = (bf16[2,6,16,256]{3,2,1,0:T(8,128)(2,1)S(1)}, bf16[2,6,16,256]{3,2,1,0:T(8,128)(2,1)S(1)}, u32[]{:S(2)}, u32[]{:S(2)}) collective-permute-start(bf16[2,6,16,256]{3,2,1,0:T(8,128)(2,1)S(1)} %fusion.3), channel_id=1, source_target_pairs={{0,0},{1,8},{2,16},{3,24},{4,32},{5,40},{6,48},{7,56},{8,64},{9,72... | collective-permute-start | bytes 294920 | tf_op jit(solution)/shard_map/ppermute | solution.py:306
  39.4 0.1 select_bitcast_fusion.1
  39.6 0.1 pad_maximum_fusion.row_mine
  39.6 2.2 %collective-permute-start.9 = (bf16[2,4,12,16,256]{4,3,2,1,0:T(8,128)(2,1)S(1)}, bf16[2,4,12,16,256]{4,3,2,1,0:T(8,128)(2,1)S(1)}, u32[]{:S(2)}, u32[]{:S(2)}) collective-permute-start(bf16[2,4,12,16,256]{4,3,2,1,0:T(8,128)(2,1)S(1)} %pad_maximum_fusion.row_mine), channel_id=1, source_target_pairs={{0,12},{1,13},{2,14},{3,15},{4,8},{5,9},{6,10},{7,11},{8,4},{9,5},... | collective-permute-start | bytes 2359304 | tf_op jit(solution)/shard_map/ppermute | solution.py:255
  41.8 0.0 collective-permute-done.10.other
  41.8 5.2 %factor_start.1 = (bf16[512,256]{1,0:T(8,128)(2,1)S(1)}, f32[128,128]{1,0:T(8,128)S(1)}, f32[128,128]{1,0:T(8,128)S(1)}, f32[128,128]{1,0:T(8,128)S(1)}) custom-call(s32[2]{0:T(128)S(1)} %pad_add_fusion.pos, bf16[2,4,2,16,256]{4,3,2,1,0:T(8,128)(2,1)S(1)} %pad_maximum_fusion.5.mine, bf16[2,4,2,16,256]{4,3,2,1,0:T(8,128)(2,1)S(1)} %collective-permute-done.10.other), custom_call_target="tpu_custom_call" | custom-call | flops 4000000000 | bytes 1000000 | tf_op jit(solution)/shard_map/factor_start/pallas_call | solution.py:144
  47.0 0.0 collective-permute-done.11
  47.0 1.8 %collective-permute-start.12 = (bf16[2,6,16,256]{3,2,1,0:T(8,128)(2,1)S(1)}, bf16[2,6,16,256]{3,2,1,0:T(8,128)(2,1)S(1)}, u32[]{:S(2)}, u32[]{:S(2)}) collective-permute-start(bf16[2,6,16,256]{3,2,1,0:T(8,128)(2,1)S(1)} %collective-permute-done.11), channel_id=1, source_target_pairs={{0,32},{16,48},{32,0},{48,16},{64,96},{80,112},{96,64},{112,80},{1... | collective-permute-start | bytes 294920 | tf_op jit(solution)/shard_map/ppermute | solution.py:250
  48.8 4.9 %factor_middle.1 = (bf16[256,768]{1,0:T(8,128)(2,1)S(1)}, f32[256,256]{1,0:T(8,128)S(1)}, f32[256,256]{1,0:T(8,128)S(1)}) custom-call(bf16[512,256]{1,0:T(8,128)(2,1)S(1)} %get-tuple-element.37.u0, f32[128,128]{1,0:T(8,128)S(1)} %get-tuple-element.38.top, f32[128,128]{1,0:T(8,128)S(1)} %get-tuple-element.39.w, f32[128,128]{1,0:T(8,128)S(1)} %get-tuple-element.40.rest), custom_call_target="tpu_custom_call" | custom-call | flops 4000000000 | bytes 1000000 | tf_op jit(solution)/shard_map/factor_middle/pallas_call | solution.py:144
  53.6 0.0 collective-permute-done.12
  53.7 0.9 collective-permute-start.13
  54.6 4.3 %factor_next.1 = (f32[128,128]{1,0:T(8,128)S(1)}, f32[128,128]{1,0:T(8,128)S(1)}, f32[128,128]{1,0:T(8,128)S(1)}) custom-call(f32[256,256]{1,0:T(8,128)S(1)} %get-tuple-element.43.d1), custom_call_target="tpu_custom_call" | custom-call | flops 4000000000 | bytes 1000000 | tf_op jit(solution)/shard_map/factor_next/pallas_call | solution.py:144
  58.9 2.6 %collective-permute-done.13 = bf16[2,2,6,16,256]{4,3,2,1,0:T(8,128)(2,1)S(1)} collective-permute-done((bf16[2,2,6,16,256]{4,3,2,1,0:T(8,128)(2,1)S(1)}, bf16[2,2,6,16,256]{4,3,2,1,0:T(8,128)(2,1)S(1)}, u32[]{:S(2)}, u32[]{:S(2)}) %collective-permute-start.13) | collective-permute-done | bytes 196640 | tf_op jit(solution)/shard_map/ppermute | solution.py:250
  61.6 1.1 %collective-permute-start.14 = (bf16[4,2,6,16,256]{4,3,2,1,0:T(8,128)(2,1)S(1)}, bf16[4,2,6,16,256]{4,3,2,1,0:T(8,128)(2,1)S(1)}, u32[]{:S(2)}, u32[]{:S(2)}) collective-permute-start(bf16[4,2,6,16,256]{4,3,2,1,0:T(8,128)(2,1)S(1)} %bitcast.70), channel_id=1, source_target_pairs={{0,16},{16,0},{32,48},{48,32},{64,80},{80,64},{96,112},{112,96},{1... | collective-permute-start | bytes 1179656 | tf_op jit(solution)/shard_map/ppermute | solution.py:250
  62.6 4.5 %factor_end.1.x1 = bf16[256,1536]{1,0:T(8,128)(2,1)S(1)} custom-call(f32[128,128]{1,0:T(8,128)S(1)} %get-tuple-element.50.top, f32[128,128]{1,0:T(8,128)S(1)} %get-tuple-element.51.w, f32[128,128]{1,0:T(8,128)S(1)} %get-tuple-element.52.rest, f32[256,256]{1,0:T(8,128)S(1)} %get-tuple-element.53.lx), custom_call_target="tpu_custom_call" | custom-call | flops 4000000000 | bytes 1000000 | tf_op jit(solution)/shard_map/factor_end/pallas_call | solution.py:144
  67.2 0.0 collective-permute-done.9.row_other
  67.2 0.0 collective-permute-done.14.col_other
  67.2 30.0 %schur.1 = (f32[36864,128]{1,0:T(8,128)}, f32[12,256,512]{2,1,0:T(8,128)}) custom-call(s32[2]{0:T(128)S(1)} %pad_add_fusion.pos, bf16[2,4,12,16,256]{4,3,2,1,0:T(8,128)(2,1)S(1)} %pad_maximum_fusion.row_mine, bf16[2,4,12,16,256]{4,3,2,1,0:T(8,128)(2,1)S(1)} %collective-permute-done.9.row_other, bf16[4,2,6,16,256]{4,3,2,1,0:T(8,128)(2,1)S(1)} %bitcast.71, ...), custom_call_target="tpu_custom_call" | custom-call | flops 24000000000 | bytes 30000000 | tf_op jit(solution)/shard_map/schur/pallas_call | solution.py:226
  (17 shorter events, 0.3 us)
Async XLA Ops:
  1.3 2.8 %collective-permute-start = (bf16[16,256]{1,0:T(8,128)(2,1)S(1)}, bf16[16,256]{1,0:T(8,128)(2,1)S(1)}, u32[]{:S(2)}, u32[]{:S(2)}) collective-permute-start(bf16[16,256]{1,0:T(8,128)(2,1)S(1)} %slice_bitcast_fusion), channel_id=1, source_target_pairs={{0,16},{16,0},{32,48},{48,32},{64,80},{80,64},{96,112},{112,96},{1... | collective-permute-start | bytes 24584 | tf_op jit(solution)/shard_map/ppermute | solution.py:250
  2.8 5.0 %collective-permute-start.2 = (bf16[12,16,256]{2,1,0:T(8,128)(2,1)}, bf16[12,16,256]{2,1,0:T(8,128)(2,1)S(1)}, u32[]{:S(2)}, u32[]{:S(2)}) collective-permute-start(bf16[12,16,256]{2,1,0:T(8,128)(2,1)} %bitcast.80), channel_id=1, source_target_pairs={{0,1},{1,0},{2,3},{3,2},{4,5},{5,4},{6,7},{7,6},{8,9},{9,8},{10,11... | collective-permute-start | bytes 294920 | tf_op jit(solution)/shard_map/ppermute | solution.py:255
  4.9 2.9 %collective-permute-start.1 = (bf16[2,16,256]{2,1,0:T(8,128)(2,1)S(1)}, bf16[2,16,256]{2,1,0:T(8,128)(2,1)S(1)}, u32[]{:S(2)}, u32[]{:S(2)}) collective-permute-start(bf16[2,16,256]{2,1,0:T(8,128)(2,1)S(1)} %pad_maximum_fusion.9), channel_id=1, source_target_pairs={{0,32},{16,48},{32,0},{48,16},{64,96},{80,112},{96,64},{112,80},{1... | collective-permute-start | bytes 49160 | tf_op jit(solution)/shard_map/ppermute | solution.py:250
  7.8 7.2 %collective-permute-start.3 = (bf16[2,16,256]{2,1,0:T(8,128)(2,1)S(1)}, bf16[2,16,256]{2,1,0:T(8,128)(2,1)S(1)}, u32[]{:S(2)}, u32[]{:S(2)}) collective-permute-start(bf16[2,16,256]{2,1,0:T(8,128)(2,1)S(1)} %broadcast_select_fusion.2), channel_id=1, source_target_pairs={{0,96},{16,112},{32,64},{48,80},{64,32},{80,48},{96,0},{112,16},{1... | collective-permute-start | bytes 49160 | tf_op jit(solution)/shard_map/ppermute | solution.py:250
  12.6 6.3 %collective-permute-start.4 = (bf16[2,12,16,256]{3,2,1,0:T(8,128)(2,1)S(1)}, bf16[2,12,16,256]{3,2,1,0:T(8,128)(2,1)S(1)}, u32[]{:S(2)}, u32[]{:S(2)}) collective-permute-start(bf16[2,12,16,256]{3,2,1,0:T(8,128)(2,1)S(1)} %pad_maximum_fusion.3), channel_id=1, source_target_pairs={{0,3},{1,2},{2,1},{3,0},{4,7},{5,6},{6,5},{7,4},{8,11},{9,10},{10,... | collective-permute-start | bytes 589832 | tf_op jit(solution)/shard_map/ppermute | solution.py:255
  18.8 2.6 %collective-permute-start.5 = (bf16[2,16,256]{2,1,0:T(8,128)(2,1)S(1)}, bf16[2,16,256]{2,1,0:T(8,128)(2,1)S(1)}, u32[]{:S(2)}, u32[]{:S(2)}) collective-permute-start(bf16[2,16,256]{2,1,0:T(8,128)(2,1)S(1)} %broadcast_select_fusion.3), channel_id=1, source_target_pairs={{0,1},{1,0},{2,3},{3,2},{4,5},{5,4},{6,7},{7,6},{8,9},{9,8},{10,11... | collective-permute-start | bytes 49160 | tf_op jit(solution)/shard_map/ppermute | solution.py:255
  21.4 4.1 %collective-permute-start.6 = (bf16[2,2,16,256]{3,2,1,0:T(8,128)(2,1)S(1)}, bf16[2,2,16,256]{3,2,1,0:T(8,128)(2,1)S(1)}, u32[]{:S(2)}, u32[]{:S(2)}) collective-permute-start(bf16[2,2,16,256]{3,2,1,0:T(8,128)(2,1)S(1)} %pad_maximum_fusion.8), channel_id=1, source_target_pairs={{0,3},{1,2},{2,1},{3,0},{4,7},{5,6},{6,5},{7,4},{8,11},{9,10},{10,... | collective-permute-start | bytes 98312 | tf_op jit(solution)/shard_map/ppermute | solution.py:255
  24.0 6.7 %collective-permute-start.8 = (bf16[4,12,16,256]{3,2,1,0:T(8,128)(2,1)S(1)}, bf16[4,12,16,256]{3,2,1,0:T(8,128)(2,1)S(1)}, u32[]{:S(2)}, u32[]{:S(2)}) collective-permute-start(bf16[4,12,16,256]{3,2,1,0:T(8,128)(2,1)S(1)} %bitcast.72), channel_id=1, source_target_pairs={{0,4},{1,5},{2,6},{3,7},{4,0},{5,1},{6,2},{7,3},{8,12},{9,13},{10,... | collective-permute-start | bytes 1179656 | tf_op jit(solution)/shard_map/ppermute | solution.py:255
  25.5 4.4 %collective-permute-start.7 = (bf16[4,2,16,256]{3,2,1,0:T(8,128)(2,1)S(1)}, bf16[4,2,16,256]{3,2,1,0:T(8,128)(2,1)S(1)}, u32[]{:S(2)}, u32[]{:S(2)}) collective-permute-start(bf16[4,2,16,256]{3,2,1,0:T(8,128)(2,1)S(1)} %bitcast.79), channel_id=1, source_target_pairs={{0,12},{1,13},{2,14},{3,15},{4,8},{5,9},{6,10},{7,11},{8,4},{9,5},... | collective-permute-start | bytes 196616 | tf_op jit(solution)/shard_map/ppermute | solution.py:255
  30.7 11.2 %collective-permute-start.10 = (bf16[2,4,2,16,256]{4,3,2,1,0:T(8,128)(2,1)S(1)}, bf16[2,4,2,16,256]{4,3,2,1,0:T(8,128)(2,1)S(1)}, u32[]{:S(2)}, u32[]{:S(2)}) collective-permute-start(bf16[2,4,2,16,256]{4,3,2,1,0:T(8,128)(2,1)S(1)} %pad_maximum_fusion.5.mine), channel_id=1, source_target_pairs={{0,4},{1,5},{2,6},{3,7},{4,0},{5,1},{6,2},{7,3},{8,12},{9,13},{10,... | collective-permute-start | bytes 393224 | tf_op jit(solution)/shard_map/ppermute | solution.py:255
  31.9 15.1 %collective-permute-start.11 = (bf16[2,6,16,256]{3,2,1,0:T(8,128)(2,1)S(1)}, bf16[2,6,16,256]{3,2,1,0:T(8,128)(2,1)S(1)}, u32[]{:S(2)}, u32[]{:S(2)}) collective-permute-start(bf16[2,6,16,256]{3,2,1,0:T(8,128)(2,1)S(1)} %fusion.3), channel_id=1, source_target_pairs={{0,0},{1,8},{2,16},{3,24},{4,32},{5,40},{6,48},{7,56},{8,64},{9,72... | collective-permute-start | bytes 294920 | tf_op jit(solution)/shard_map/ppermute | solution.py:306
  39.6 27.5 %collective-permute-start.9 = (bf16[2,4,12,16,256]{4,3,2,1,0:T(8,128)(2,1)S(1)}, bf16[2,4,12,16,256]{4,3,2,1,0:T(8,128)(2,1)S(1)}, u32[]{:S(2)}, u32[]{:S(2)}) collective-permute-start(bf16[2,4,12,16,256]{4,3,2,1,0:T(8,128)(2,1)S(1)} %pad_maximum_fusion.row_mine), channel_id=1, source_target_pairs={{0,12},{1,13},{2,14},{3,15},{4,8},{5,9},{6,10},{7,11},{8,4},{9,5},... | collective-permute-start | bytes 2359304 | tf_op jit(solution)/shard_map/ppermute | solution.py:255
  47.0 6.6 %collective-permute-start.12 = (bf16[2,6,16,256]{3,2,1,0:T(8,128)(2,1)S(1)}, bf16[2,6,16,256]{3,2,1,0:T(8,128)(2,1)S(1)}, u32[]{:S(2)}, u32[]{:S(2)}) collective-permute-start(bf16[2,6,16,256]{3,2,1,0:T(8,128)(2,1)S(1)} %collective-permute-done.11), channel_id=1, source_target_pairs={{0,32},{16,48},{32,0},{48,16},{64,96},{80,112},{96,64},{112,80},{1... | collective-permute-start | bytes 294920 | tf_op jit(solution)/shard_map/ppermute | solution.py:250
  53.7 7.8 %collective-permute-start.13 = (bf16[2,2,6,16,256]{4,3,2,1,0:T(8,128)(2,1)S(1)}, bf16[2,2,6,16,256]{4,3,2,1,0:T(8,128)(2,1)S(1)}, u32[]{:S(2)}, u32[]{:S(2)}) collective-permute-start(bf16[2,2,6,16,256]{4,3,2,1,0:T(8,128)(2,1)S(1)} %pad_maximum_fusion.4), channel_id=1, source_target_pairs={{0,96},{16,112},{32,64},{48,80},{64,32},{80,48},{96,0},{112,16},{1... | collective-permute-start | bytes 589832 | tf_op jit(solution)/shard_map/ppermute | solution.py:250
  61.6 5.6 %collective-permute-start.14 = (bf16[4,2,6,16,256]{4,3,2,1,0:T(8,128)(2,1)S(1)}, bf16[4,2,6,16,256]{4,3,2,1,0:T(8,128)(2,1)S(1)}, u32[]{:S(2)}, u32[]{:S(2)}) collective-permute-start(bf16[4,2,6,16,256]{4,3,2,1,0:T(8,128)(2,1)S(1)} %bitcast.70), channel_id=1, source_target_pairs={{0,16},{16,0},{32,48},{48,32},{64,80},{80,64},{96,112},{112,96},{1... | collective-permute-start | bytes 1179656 | tf_op jit(solution)/shard_map/ppermute | solution.py:250
